TPU v7x, 32 devices: a whole 2x2x4 slice. The times are simulated.
32 devices in a mesh: seq: 8 (over z, x), dp: 4 (over y, core).
Axes of the slice: x: 2, y: 2, z: 4, core: 2. Of those that a mesh axis runs over, the one named last changes fastest.
Arguments:
- layer_input: bfloat16 [16384, 576], P(('seq', 'dp')), may hold values from -6 to 6
- w_qkv: bfloat16 [552960], P(('seq', 'dp')), may hold values from -0.25 to 0.25
- w_out: bfloat16 [331776], P(('seq', 'dp')), may hold values from -4 to 4
- w_gu: bfloat16 [1769472], P(('seq', 'dp')), may hold values from -0.25 to 0.25
- w_down: bfloat16 [884736], P(('seq', 'dp')), may hold values from -0.15625 to 0.15625
- norm_gains: float32 [2, 576], replicated, may hold values from 0.1 to 1.9
- lengths: int32 [4, 6], P('dp'), may hold values from 1 to 2048, 4096 in all within a row
- cotangent: bfloat16 [16384, 576], P(('seq', 'dp')), may hold values from -6 to 6
Outputs:
- layer_output: bfloat16 [16384, 576], P(('seq', 'dp'))
- input_grad: float32 [16384, 576], P(('seq', 'dp'))
- g_qkv: float32 [552960], P(('seq', 'dp'))
- g_out: float32 [331776], P(('seq', 'dp'))
- g_gu: float32 [1769472], P(('seq', 'dp'))
- g_down: float32 [884736], P(('seq', 'dp'))
- gains_grad: float32 [2, 576], replicated
Inputs may be any that keep to these rules, and one draw needn't show every extreme that they name: Each row lists the lengths of the 6 sequences of one dp group in order; a row sums to 4096, and its largest entry is exactly 2048.
All inputs are finite; a program needn't handle non-finite values.
Results may differ from a plain program's by a relative error of at most 0.012.
Values may be sent and summed in bfloat16 or wider, within the bound.
A program may use at most 128 MiB of HBM per device.

v0:
```python
import math

import jax
import jax.numpy as jnp
from jax import lax
from jax.sharding import PartitionSpec as P

D = 576
QUERY_HEADS = 9
KEY_VALUE_HEADS = 3
HEAD_SIZE = 64
FF = 1536


EPS = 1e-05
THETA = 100000.0
MASKED = -1e30


def rms_norm(value_rows, gain):
    return (
        value_rows
        * lax.rsqrt(jnp.mean(value_rows * value_rows, axis=-1, keepdims=True) + EPS)
        * gain
    )


def apply_rotary(value_rows, token_position):
    half = value_rows.shape[-1] // 2
    freq = jnp.exp(
        jnp.arange(half, dtype=jnp.float32) * (-2.0 * math.log(THETA) / value_rows.shape[-1])
    )
    angle = token_position.astype(jnp.float32)[:, None] * freq[None, :]
    cosine = jnp.cos(angle)[:, None, :]
    sine = jnp.sin(angle)[:, None, :]
    first = value_rows[..., :half]
    second = value_rows[..., half:]
    return jnp.concatenate(
        [first * cosine - second * sine, second * cosine + first * sine], axis=-1
    )


def layout(lengths_row, index):
    ends = jnp.cumsum(lengths_row, dtype=jnp.int32)
    done = ends[None, :] <= index[:, None]
    segment_index = jnp.sum(done.astype(jnp.int32), axis=1, dtype=jnp.int32)
    token_position = index - jnp.sum(
        jnp.where(done, lengths_row[None, :], 0), axis=1, dtype=jnp.int32
    )
    return (segment_index, token_position)


def silu_product(gate_up):
    width = gate_up.shape[1] // 2
    return jax.nn.silu(gate_up[:, :width]) * gate_up[:, width:]


def per_device(layer_input, w_qkv, w_out, w_gu, w_down, norm_gains, lengths, cotangent):
    token_rows = layer_input.shape[0]
    seq_count = lax.axis_size("seq")
    group = token_rows * seq_count
    heads_per_group = QUERY_HEADS // KEY_VALUE_HEADS
    query_width = QUERY_HEADS * HEAD_SIZE
    key_width = KEY_VALUE_HEADS * HEAD_SIZE
    scale = 1.0 / math.sqrt(HEAD_SIZE)
    block_current = math.gcd(group, 512)
    blocks = group // block_current
    numbers = jnp.arange(blocks, dtype=jnp.int32)

    def fetch_weights():
        parts = (
            lax.all_gather(w_qkv, ("seq", "dp"), axis=0, tiled=True),
            lax.all_gather(w_out, ("seq", "dp"), axis=0, tiled=True),
            lax.all_gather(w_gu, ("seq", "dp"), axis=0, tiled=True),
            lax.all_gather(w_down, ("seq", "dp"), axis=0, tiled=True),
        )
        return (
            parts[0].reshape(D, -1),
            parts[1].reshape(query_width, D),
            parts[2].reshape(D, 2 * FF),
            parts[3].reshape(FF, D),
        )

    def fetch_pairs(keys_mine, values_mine):
        return (
            lax.all_gather(keys_mine, "seq", axis=0, tiled=True),
            lax.all_gather(values_mine, "seq", axis=0, tiled=True),
        )

    lengths_row = lengths[0]
    query_index = lax.axis_index("seq") * token_rows + jnp.arange(token_rows, dtype=jnp.int32)
    query_segment, query_token_position = layout(lengths_row, query_index)
    key_index = jnp.arange(group, dtype=jnp.int32)
    key_valid = key_index >= 0
    key_segment = layout(lengths_row, jnp.maximum(key_index, 0))[0]

    def block_parts(key_value_pairs, number):
        start_offset = number * block_current
        key_window_part = lax.dynamic_slice_in_dim(
            key_value_pairs[0], start_offset, block_current, 0
        ).reshape(block_current, KEY_VALUE_HEADS, HEAD_SIZE)
        value_window_part = lax.dynamic_slice_in_dim(
            key_value_pairs[1], start_offset, block_current, 0
        ).reshape(block_current, KEY_VALUE_HEADS, HEAD_SIZE)
        seg_slice = lax.dynamic_slice_in_dim(key_segment, start_offset, block_current, 0)
        idx_slice = lax.dynamic_slice_in_dim(key_index, start_offset, block_current, 0)
        valid_slice = lax.dynamic_slice_in_dim(key_valid, start_offset, block_current, 0)
        allowed = (
            valid_slice[None, :]
            & (query_segment[:, None] == seg_slice[None, :])
            & (query_index[:, None] >= idx_slice[None, :])
        )
        return (key_window_part, value_window_part, allowed[None, None])

    mixing_in, mixing_out, expand_matrix, shrink_matrix = fetch_weights()
    inputs = layer_input.astype(jnp.float32)
    normed, norm_back = jax.vjp(rms_norm, inputs, norm_gains[0])
    normed_low = normed.astype(jnp.bfloat16)
    projected_output = jnp.dot(normed_low, mixing_in, preferred_element_type=jnp.float32)
    rotated_query, query_unrot = jax.vjp(
        lambda part: apply_rotary(
            part.reshape(token_rows, QUERY_HEADS, HEAD_SIZE), query_token_position
        ),
        projected_output[:, :query_width],
    )
    keys_rot, unrotated_keys = jax.vjp(
        lambda part: apply_rotary(
            part.reshape(token_rows, KEY_VALUE_HEADS, HEAD_SIZE), query_token_position
        ),
        projected_output[:, query_width : query_width + key_width],
    )
    query_lower_precision = rotated_query.astype(jnp.bfloat16).reshape(
        token_rows, KEY_VALUE_HEADS, heads_per_group, HEAD_SIZE
    )
    keys_low = keys_rot.astype(jnp.bfloat16).reshape(token_rows, key_width)
    values_low = projected_output[:, query_width + key_width :].astype(jnp.bfloat16)
    pairs_now = fetch_pairs(keys_low, values_low)

    def scores_of(key_window_part, allowed):
        raw = (
            jnp.einsum(
                "tkgd,skd->kgts",
                query_lower_precision,
                key_window_part,
                preferred_element_type=jnp.float32,
            )
            * scale
        )
        return jnp.where(allowed, raw, MASKED)

    statistic_dims = (KEY_VALUE_HEADS, heads_per_group, token_rows)

    def stat_step(carry, number):
        key_window_part, value_window_part, allowed = block_parts(pairs_now, number)
        scores = scores_of(key_window_part, allowed)
        highest = jnp.maximum(carry[0], jnp.max(scores, axis=-1))
        summed = carry[1] * jnp.exp(carry[0] - highest) + jnp.sum(
            jnp.where(allowed, jnp.exp(scores - highest[..., None]), 0.0), axis=-1
        )
        return ((highest, summed), None)

    stats = lax.scan(
        stat_step,
        (jnp.full(statistic_dims, MASKED, jnp.float32), jnp.zeros(statistic_dims, jnp.float32)),
        numbers,
    )[0]
    log_total = stats[0] + jnp.log(stats[1])

    def probs_of(key_value_pairs, number):
        key_window_part, value_window_part, allowed = block_parts(key_value_pairs, number)
        scores = scores_of(key_window_part, allowed)
        probs = jnp.where(allowed, jnp.exp(scores - log_total[..., None]), 0.0)
        return (key_window_part, value_window_part, probs)

    def out_step(summed, number):
        key_window_part, value_window_part, probs = probs_of(pairs_now, number)
        return (
            summed
            + jnp.einsum(
                "kgts,skd->tkgd",
                probs.astype(jnp.bfloat16),
                value_window_part,
                preferred_element_type=jnp.float32,
            ),
            None,
        )

    head_layout_dims = (token_rows, KEY_VALUE_HEADS, heads_per_group, HEAD_SIZE)
    attended_rows = lax.scan(out_step, jnp.zeros(head_layout_dims, jnp.float32), numbers)[0]
    attended_low = attended_rows.reshape(token_rows, query_width).astype(jnp.bfloat16)
    mid = inputs + jnp.dot(attended_low, mixing_out, preferred_element_type=jnp.float32)
    normed_two, norm_two_back = jax.vjp(rms_norm, mid, norm_gains[1])
    normed_two_low = normed_two.astype(jnp.bfloat16)
    gate_up = jnp.dot(normed_two_low, expand_matrix, preferred_element_type=jnp.float32)
    hidden, hidden_back = jax.vjp(silu_product, gate_up)
    hidden_low = hidden.astype(jnp.bfloat16)
    result = (mid + jnp.dot(hidden_low, shrink_matrix, preferred_element_type=jnp.float32)).astype(
        jnp.bfloat16
    )
    mixing_in, mixing_out, expand_matrix, shrink_matrix = fetch_weights()
    pairs_back = fetch_pairs(keys_low, values_low)
    grad_down = jnp.einsum("tf,td->fd", hidden_low, cotangent, preferred_element_type=jnp.float32)
    d_hidden = jnp.einsum("td,fd->tf", cotangent, shrink_matrix, preferred_element_type=jnp.float32)
    d_gate_up = hidden_back(d_hidden)[0].astype(jnp.bfloat16)
    grad_expand = jnp.einsum(
        "td,tf->df", normed_two_low, d_gate_up, preferred_element_type=jnp.float32
    )
    d_normed_two = jnp.einsum(
        "tf,df->td", d_gate_up, expand_matrix, preferred_element_type=jnp.float32
    )
    d_mid_part, grad_gain_two = norm_two_back(d_normed_two)
    d_mid = cotangent.astype(jnp.float32) + d_mid_part
    d_branch = d_mid.astype(jnp.bfloat16)
    grad_mixing_out = jnp.einsum(
        "tq,td->qd", attended_low, d_branch, preferred_element_type=jnp.float32
    )
    d_attended = (
        jnp.einsum("td,qd->tq", d_branch, mixing_out, preferred_element_type=jnp.float32)
        .astype(jnp.bfloat16)
        .reshape(head_layout_dims)
    )
    delta = jnp.sum(d_attended.astype(jnp.float32) * attended_rows, axis=-1).transpose(1, 2, 0)

    def grad_step(d_query, number):
        key_window_part, value_window_part, probs = probs_of(pairs_back, number)
        d_probs = jnp.einsum(
            "tkgd,skd->kgts", d_attended, value_window_part, preferred_element_type=jnp.float32
        )
        d_scores = (probs * (d_probs - delta[..., None])).astype(jnp.bfloat16)
        new_query = (
            d_query
            + jnp.einsum(
                "kgts,skd->tkgd", d_scores, key_window_part, preferred_element_type=jnp.float32
            )
            * scale
        )
        d_keys = (
            jnp.einsum(
                "kgts,tkgd->skd",
                d_scores,
                query_lower_precision,
                preferred_element_type=jnp.float32,
            )
            * scale
        )
        d_values = jnp.einsum(
            "kgts,tkgd->skd",
            probs.astype(jnp.bfloat16),
            d_attended,
            preferred_element_type=jnp.float32,
        )
        return (
            new_query,
            (d_keys.reshape(block_current, key_width), d_values.reshape(block_current, key_width)),
        )

    d_query, key_value_rows = lax.scan(grad_step, jnp.zeros(head_layout_dims, jnp.float32), numbers)
    local_key_gradient = lax.psum_scatter(
        key_value_rows[0].reshape(group, key_width).astype(jnp.bfloat16),
        "seq",
        scatter_dimension=0,
        tiled=True,
    ).astype(jnp.float32)
    d_values_mine = lax.psum_scatter(
        key_value_rows[1].reshape(group, key_width).astype(jnp.bfloat16),
        "seq",
        scatter_dimension=0,
        tiled=True,
    ).astype(jnp.float32)
    d_query_pre = query_unrot(d_query.reshape(token_rows, QUERY_HEADS, HEAD_SIZE))[0]
    prior_key_gradient = unrotated_keys(
        local_key_gradient.reshape(token_rows, KEY_VALUE_HEADS, HEAD_SIZE)
    )[0]
    d_projected = jnp.concatenate([d_query_pre, prior_key_gradient, d_values_mine], axis=1).astype(
        jnp.bfloat16
    )
    grad_mixing_in = jnp.einsum(
        "td,tq->dq", normed_low, d_projected, preferred_element_type=jnp.float32
    )
    d_normed = jnp.einsum("tq,dq->td", d_projected, mixing_in, preferred_element_type=jnp.float32)
    d_input_part, grad_gain_one = norm_back(d_normed)
    d_input = d_mid + d_input_part
    summed_grads = (
        lax.psum_scatter(
            grad_mixing_in.reshape(-1), ("seq", "dp"), scatter_dimension=0, tiled=True
        ),
        lax.psum_scatter(
            grad_mixing_out.reshape(-1), ("seq", "dp"), scatter_dimension=0, tiled=True
        ),
        lax.psum_scatter(grad_expand.reshape(-1), ("seq", "dp"), scatter_dimension=0, tiled=True),
        lax.psum_scatter(grad_down.reshape(-1), ("seq", "dp"), scatter_dimension=0, tiled=True),
    )
    gain_grads = lax.psum(jnp.stack([grad_gain_one, grad_gain_two]), ("seq", "dp"))
    return (
        result,
        d_input,
        summed_grads[0],
        summed_grads[1],
        summed_grads[2],
        summed_grads[3],
        gain_grads,
    )


def solution(mesh):
    return jax.shard_map(
        per_device,
        mesh=mesh,
        in_specs=(
            P(("seq", "dp"), None),
            P(("seq", "dp")),
            P(("seq", "dp")),
            P(("seq", "dp")),
            P(("seq", "dp")),
            P(),
            P("dp", None),
            P(("seq", "dp"), None),
        ),
        out_specs=(
            P(("seq", "dp"), None),
            P(("seq", "dp"), None),
            P(("seq", "dp")),
            P(("seq", "dp")),
            P(("seq", "dp")),
            P(("seq", "dp")),
            P(),
        ),
        check_vma=False,
    )
```

profile of v0, /device:TPU:0, one launch (start us, length us, event | category | flops | bytes accessed | tf_op | source)
XLA Modules:
  0.0 851.0 jit_solution(7512977916440498301)
XLA Ops:
  13.5 57.5 %all-gather.16.cloned.1.call-done = bf16[32,1,17280]{2,1,0:T(2,128)(2,1)} async-done(((bf16[1,1,17280]{2,1,0:T(2,128)(2,1)}), bf16[32,1,17280]{2,1,0:T(2,128)(2,1)}) %all-gather.16.cloned.1.call-update) | async-done | bytes 1105936 | tf_op jit(solution)/shard_map/all_gather | solution.py:72
  71.0 7.7 reduce.1
  85.7 44.2 %all-gather.1 = bf16[32,1,10368]{2,1,0:T(2,128)(2,1)S(1)} all-gather(bf16[1,1,10368]{2,1,0:T(2,128)(2,1)S(1)} %reshape.464), channel_id=1, replica_groups=mesh['seq'=8,'dp'=4] {'seq','dp'}, dimensions={0}, use_global_device_ids=true | all-gather | bytes 684288 | tf_op jit(solution)/shard_map/all_gather | solution.py:73
  129.8 4.8 reduce.2
  134.6 2.8 reshape.445
  137.7 4.3 reshape.447
  142.0 35.1 %all-gather.10.cloned.1.call-done = bf16[4096,192]{0,1:T(8,128)(2,1)} async-done(((bf16[512,192]{0,1:T(8,128)(2,1)}), bf16[4096,192]{0,1:T(8,128)(2,1)}) %all-gather.10.cloned.1.call-update) | async-done | bytes 1572880 | tf_op jit(solution)/shard_map/all_gather | solution.py:86
  177.1 52.5 %while.42 = (s32[]{:T(128)}, f32[3,3,512]{2,1,0:T(4,128)S(1)}, f32[3,3,512]{2,1,0:T(4,128)S(1)}, s32[512]{0:T(512)S(1)}, s32[8]{0:T(128)S(1)}, /*index=5*/s32[40...) while((s32[]{:T(128)}, f32[3,3,512]{2,1,0:T(4,128)S(1)}, ...), condition=%wide.region_8.9_spmd.clone, body=%wide.region_5.8_spmd.clone.sunk | while | flops 321674240 | bytes 21098720 | solution.py:162
  229.6 65.2 %while.43 = (s32[]{:T(128)}, f32[512,3,3,64]{0,3,2,1:T(8,128)}, s32[8]{0:T(128)S(1)}, bf16[4096,192]{0,1:T(8,128)(2,1)}, s32[512]{0:T(512)S(1)}, /*index=5*/s32[...) while((s32[]{:T(128)}, f32[512,3,3,64]{0,3,2,1:T(8,128)}, ...), condition=%wide.region_10.11_spmd.clone, body=%wide.region_9.10_spmd.clone.sunk | while | flops 617153024 | bytes 4690153 | solution.py:189
  232.4 4.3 fusion.134
  239.4 5.6 fusion.134
  247.7 5.6 fusion.134
  256.0 5.6 fusion.134
  264.3 5.6 fusion.134
  272.6 5.6 fusion.134
  280.9 5.6 fusion.134
  289.2 5.6 fusion.134
  297.1 6.7 reshape.446
  303.8 4.9 fusion.71
  308.8 3.6 fusion.56
  312.4 2.8 multiply_reduce_fusion
  319.7 127.2 %while.44 = (s32[]{:T(128)}, f32[512,3,3,64]{0,3,2,1:T(8,128)S(1)}, bf16[8,512,192]{1,2,0:T(8,128)(2,1)}, bf16[8,512,192]{1,2,0:T(8,128)(2,1)}, s32[8]{0:T(128)S...) while((s32[]{:T(128)}, f32[512,3,3,64]{0,3,2,1:T(8,128)S(1)}, ...), condition=%wide.region_15.16_spmd.clone, body=%wide.region_14.15_spmd.clone.sunk | while | flops 1540129280 | bytes 53109092 | solution.py:257
  328.9 3.5 fusion.146
  342.3 2.5 fusion.148
  344.8 3.5 fusion.146
  360.7 3.5 fusion.146
  374.1 2.5 fusion.148
  376.6 3.5 fusion.146
  392.4 3.5 fusion.146
  405.8 2.5 fusion.148
  408.3 3.5 fusion.146
  421.6 2.5 fusion.148
  424.2 3.5 fusion.146
  440.1 3.5 fusion.146
  446.9 2.8 copy.53
  449.7 2.8 copy.54
  452.6 5.0 convolution_bitcast_fusion.1
  457.6 4.5 copy.55
  463.9 3.1 reshape.455
  467.0 4.9 fusion.73
  471.9 5.3 reshape.457
  477.6 35.8 %reduce-scatter.3.cloned.1.call-done = bf16[512,192]{0,1:T(8,128)(2,1)} async-done(((bf16[4096,192]{0,1:T(8,128)(2,1)}), bf16[512,192]{0,1:T(8,128)(2,1)}) %reduce-scatter.3.cloned.1.call-update) | async-done | bytes 196624 | tf_op jit(solution)/shard_map/reduce_scatter | solution.py:258
  514.5 67.1 %reduce-scatter.5.cloned.1.call-done = bf16[512,192]{0,1:T(8,128)(2,1)} async-done(((bf16[4096,192]{0,1:T(8,128)(2,1)}), bf16[512,192]{0,1:T(8,128)(2,1)}) %reduce-scatter.5.cloned.1.call-update) | async-done | bytes 196624 | tf_op jit(solution)/shard_map/reduce_scatter | solution.py:264
  581.6 3.2 fusion.54
  584.8 3.6 reshape.454
  589.2 4.1 fusion.46
  594.3 42.0 %psum.7 = f32[2,576]{1,0:T(2,128)} all-reduce(f32[2,576]{1,0:T(2,128)S(1)} %pad_maximum_fusion.5), channel_id=1, replica_groups=mesh['seq'=8,'dp'=4] {'seq','dp'}, use_global_device_ids=true, to_apply=%region_25.26 | all-reduce | flops 1152 | bytes 9216 | tf_op jit(solution)/shard_map/psum | solution.py:293
  637.7 199.9 %all-reduce.13.cloned.1.call-done = (f32[552960]{0:T(1024)}, f32[331776]{0:T(1024)}, f32[1769472]{0:T(1024)}, f32[884736]{0:T(1024)}) async-done(((f32[552960]{0:T(1024)}, f32[331776]{0:T(1024)}, f32[1769472]{0:T(1024)}, f32[884736]{0:T(1024)}), (f32[552960]{0:T(1024)}, f32[331776]{0:T(1024)}, f32[1769472]{0:T(1024)}, f32[884736]{0:T(1024)})) %all-reduce.13.cloned.1.call-update) | async-done | bytes 14155792
  (430 shorter events, 178.9 us)
Async XLA Ops:
  7.2 63.8 %all-gather.16.cloned.1.call-start = ((), (), s32[]{:S(2)}) async-start(), calls=%async_computation.8 | async-start | bytes 2280960 | tf_op jit(solution)/shard_map/all_gather | solution.py:72
  8.7 129.0 %all-gather.14.cloned.1.call-start = ((), (), s32[]{:S(2)}) async-start(), calls=%async_computation.5 | async-start | bytes 1824768 | tf_op jit(solution)/shard_map/all_gather | solution.py:75
  9.4 167.7 %all-gather.10.cloned.1.call-start = ((), (), s32[]{:S(2)}) async-start(), calls=%async_computation.3 | async-start | bytes 1769472 | tf_op jit(solution)/shard_map/all_gather | solution.py:86
  11.1 68.7 %copy-start.29 = (f32[576]{0:T(1024)}, f32[576]{0:T(1024)S(1)}, u32[]{:S(2)}) copy-start(f32[576]{0:T(1024)S(1)} %get-tuple-element.478) | copy-start | bytes 6916
  13.1 65.6 %copy-start.37 = (f32[512]{0:T(512)}, f32[512]{0:T(512)S(1)}, u32[]{:S(2)}) copy-start(f32[512]{0:T(512)S(1)} %fusion.51) | copy-start | bytes 6148
  13.1 66.7 %copy-start.35 = (f32[512]{0:T(512)}, f32[512]{0:T(512)S(1)}, u32[]{:S(2)}) copy-start(f32[512]{0:T(512)S(1)} %fusion.65) | copy-start | bytes 6148
  13.4 124.0 %copy-start.20 = (f32[512,32]{0,1:T(8,128)}, f32[512,32]{0,1:T(8,128)S(1)}, u32[]{:S(2)}) copy-start(f32[512,32]{0,1:T(8,128)S(1)} %get-tuple-element.574) | copy-start | bytes 196612
  13.5 124.0 %copy-start.22 = (f32[512,32]{0,1:T(8,128)}, f32[512,32]{0,1:T(8,128)S(1)}, u32[]{:S(2)}) copy-start(f32[512,32]{0,1:T(8,128)S(1)} %get-tuple-element.575) | copy-start | bytes 196612
  82.2 3.4 copy-start.34
  83.0 146.6 %all-gather.8.cloned.1.call-start = ((), (), s32[]{:S(2)}) async-start(), calls=%async_computation.2 | async-start | bytes 1769472 | tf_op jit(solution)/shard_map/all_gather | solution.py:87
  84.8 212.2 %all-gather.12.cloned.1.call-start = ((), (), s32[]{:S(2)}) async-start(), calls=%async_computation.4 | async-start | bytes 3649536 | tf_op jit(solution)/shard_map/all_gather | solution.py:74
  85.4 428.0 %reduce-scatter.3.cloned.1.call-start = ((), (), s32[]{:S(2)}) async-start(), calls=%async_computation.6 | async-start | bytes 1769472 | tf_op jit(solution)/shard_map/reduce_scatter | solution.py:258
  134.6 2.8 slice-start
  294.8 1.5 copy-start.6
  303.8 5.0 copy-start.15
  303.8 5.0 copy-start.19
  308.8 3.6 copy-start.3
  312.4 2.8 copy-start.13
  312.4 2.8 copy-start.14
  316.3 2.7 copy-start
  316.3 1.9 copy-start.10
  317.0 2.7 copy-start.17
  324.9 1.5 copy-start.18
  326.4 2.5 copy-start.31
  342.3 2.5 copy-start.31
  358.2 2.5 copy-start.31
  374.0 2.5 copy-start.31
  389.9 2.5 copy-start.31
  405.8 2.5 copy-start.31
  421.6 2.5 copy-start.31
  437.5 2.5 copy-start.31
  449.7 131.9 %reduce-scatter.5.cloned.1.call-start = ((), (), s32[]{:S(2)}) async-start(), calls=%async_computation.7 | async-start | bytes 1769472 | tf_op jit(solution)/shard_map/reduce_scatter | solution.py:264
  452.5 385.0 %all-reduce.13.cloned.1.call-start = ((), (), s32[]{:S(2)}) async-start(), calls=%async_computation.9 | async-start | bytes 28311552
  457.6 4.5 copy-start.1
  457.6 4.5 copy-start.9
  463.9 3.1 copy-start.16
  471.9 5.3 copy-start.21
  471.9 5.3 copy-start.23
  477.5 104.1 %copy-start.30 = (f32[576]{0:T(1024)S(1)}, f32[576]{0:T(1024)}, u32[]{:S(2)}) copy-start(f32[576]{0:T(1024)} %copy-done.29) | copy-start | bytes 6916
  477.5 104.1 %copy-start.36 = (f32[512]{0:T(512)S(1)}, f32[512]{0:T(512)}, u32[]{:S(2)}) copy-start(f32[512]{0:T(512)} %copy-done.35) | copy-start | bytes 6148
  477.6 107.3 %copy-start.24 = (bf16[512,9,64]{0,2,1:T(8,128)(2,1)}, bf16[512,9,64]{0,2,1:T(8,128)(2,1)S(1)}, u32[]{:S(2)}) copy-start(bf16[512,9,64]{0,2,1:T(8,128)(2,1)S(1)} %add_convert_fusion.1) | copy-start | bytes 1769476
  514.4 70.4 %copy-start.26 = (bf16[512,3,64]{0,2,1:T(8,128)(2,1)}, bf16[512,3,64]{0,2,1:T(8,128)(2,1)S(1)}, u32[]{:S(2)}) copy-start(bf16[512,3,64]{0,2,1:T(8,128)(2,1)S(1)} %add_convert_fusion.5) | copy-start | bytes 589828
  589.1 4.1 copy-start.12
  589.1 4.1 copy-start.25
  589.1 4.1 copy-start.27
  589.1 4.1 copy-start.40
  593.3 43.0 %copy-start.38 = (f32[512]{0:T(512)S(1)}, f32[512]{0:T(512)}, u32[]{:S(2)}) copy-start(f32[512]{0:T(512)} %copy-done.37) | copy-start | bytes 6148
  593.3 43.1 %copy-start.2 = (f32[512,576]{0,1:T(8,128)S(1)}, f32[512,576]{0,1:T(8,128)}, u32[]{:S(2)}) copy-start(f32[512,576]{0,1:T(8,128)} %copy-done) | copy-start | bytes 3538948
  (23 other events, 30.8 us)
Sparse Core Ops, SparseCore 0:
  11.4 59.5 all-gather.15
  73.8 55.3 all-gather.13
  131.9 45.1 all-gather.9
  179.6 43.4 all-gather.7
  225.8 58.3 all-gather.11
  449.8 63.5 reduce-scatter.2
  517.2 64.3 reduce-scatter.4
  588.6 248.9 all-reduce.12
where the time goes:
time: 861 us; the launch traced here: 851 us
  waiting for transfers between devices  397 us (46%)
  matrix products  169 us (20%)
  local copies, waits for them, and re-layouts  119 us (14%)
  blocking collectives  86.2 us (10%)
  other arithmetic  47.2 us (5%)
  loops' own time  17.4 us (2%)
  between operations  15 us (2%)
    unnamed x9, waiting for transfers between devices  201 us
    reduce_scatter x1, waiting for transfers between devices, per_device(): lax.psum_scatter(key_value_rows[1].reshape(group, key_width).astype(jnp.b...  67.1 us
    all_gather x1, waiting for transfers between devices, fetch_weights(): lax.all_gather(w_qkv, ('seq', 'dp'), axis=0, tiled=True)  57.5 us
    all_gather x1, blocking collectives, fetch_weights(): lax.all_gather(w_out, ('seq', 'dp'), axis=0, tiled=True)  44.2 us
    dot_general x8, matrix products, out_step(): jnp.einsum('kgts,skd->tkgd', probs.astype(jnp.bfloat16), value_window_par...  43.2 us
    psum x1, blocking collectives, per_device(): lax.psum(jnp.stack([grad_gain_one, grad_gain_two]), ('seq', 'dp'))  42 us
    reduce_scatter x1, waiting for transfers between devices, per_device(): lax.psum_scatter(key_value_rows[0].reshape(group, key_width).astype(jnp.b...  35.8 us
    all_gather x1, waiting for transfers between devices, fetch_pairs(): lax.all_gather(keys_mine, 'seq', axis=0, tiled=True)  35.1 us
  transfers between devices with their start and end apart: 8, of which 5 were waited for; matrix products, arithmetic and copies ran while one was open for 20% of the time, Pallas kernels for 0%

commit v1 on v0

--- a/solution.py
+++ b/solution.py
@@ -41,7 +41,9 @@
 
 
 def layout(lengths_row, index):
-    ends = jnp.cumsum(lengths_row, dtype=jnp.int32)
+    count = lengths_row.shape[0]
+    earlier = jnp.arange(count)[:, None] >= jnp.arange(count)[None, :]
+    ends = jnp.sum(jnp.where(earlier, lengths_row[None, :], 0), axis=1, dtype=jnp.int32)
     done = ends[None, :] <= index[:, None]
     segment_index = jnp.sum(done.astype(jnp.int32), axis=1, dtype=jnp.int32)
     token_position = index - jnp.sum(

time: 861 us -> 861 us (level)
  no operation moved by 1% of the time
where the time goes in v1:
time: 861 us; the launch traced here: 851 us
  waiting for transfers between devices  397 us (46%)
  matrix products  169 us (20%)
  local copies, waits for them, and re-layouts  119 us (14%)
  blocking collectives  86.2 us (10%)
  other arithmetic  47.1 us (5%)
  loops' own time  17.4 us (2%)
  between operations  15 us (2%)
    unnamed x9, waiting for transfers between devices  201 us
    reduce_scatter x1, waiting for transfers between devices, per_device(): lax.psum_scatter(key_value_rows[1].reshape(group, key_width).astype(jnp.b...  67.1 us
    all_gather x1, waiting for transfers between devices, fetch_weights(): lax.all_gather(w_qkv, ('seq', 'dp'), axis=0, tiled=True)  57.6 us
    all_gather x1, blocking collectives, fetch_weights(): lax.all_gather(w_out, ('seq', 'dp'), axis=0, tiled=True)  44.2 us
    dot_general x8, matrix products, out_step(): jnp.einsum('kgts,skd->tkgd', probs.astype(jnp.bfloat16), value_window_par...  43.2 us
    psum x1, blocking collectives, per_device(): lax.psum(jnp.stack([grad_gain_one, grad_gain_two]), ('seq', 'dp'))  42 us
    reduce_scatter x1, waiting for transfers between devices, per_device(): lax.psum_scatter(key_value_rows[0].reshape(group, key_width).astype(jnp.b...  35.8 us
    all_gather x1, waiting for transfers between devices, fetch_pairs(): lax.all_gather(keys_mine, 'seq', axis=0, tiled=True)  35.1 us
  transfers between devices with their start and end apart: 8, of which 5 were waited for; matrix products, arithmetic and copies ran while one was open for 20% of the time, Pallas kernels for 0%

profile of v1, /device:TPU:0, one launch (start us, length us, event | category | flops | bytes accessed | tf_op | source)
XLA Modules:
  0.0 851.0 jit_solution(7654661072459942161)
XLA Ops:
  13.4 57.6 %all-gather.16.cloned.1.call-done = bf16[32,1,17280]{2,1,0:T(2,128)(2,1)} async-done(((bf16[1,1,17280]{2,1,0:T(2,128)(2,1)}), bf16[32,1,17280]{2,1,0:T(2,128)(2,1)}) %all-gather.16.cloned.1.call-update) | async-done | bytes 1105936 | tf_op jit(solution)/shard_map/all_gather | solution.py:74
  71.0 7.7 reduce.1
  85.7 44.2 %all-gather.1 = bf16[32,1,10368]{2,1,0:T(2,128)(2,1)S(1)} all-gather(bf16[1,1,10368]{2,1,0:T(2,128)(2,1)S(1)} %reshape.439), channel_id=1, replica_groups=mesh['seq'=8,'dp'=4] {'seq','dp'}, dimensions={0}, use_global_device_ids=true | all-gather | bytes 684288 | tf_op jit(solution)/shard_map/all_gather | solution.py:75
  129.8 4.8 reduce.2
  134.6 2.8 reshape.420
  137.7 4.3 reshape.422
  142.0 35.1 %all-gather.10.cloned.1.call-done = bf16[4096,192]{0,1:T(8,128)(2,1)} async-done(((bf16[512,192]{0,1:T(8,128)(2,1)}), bf16[4096,192]{0,1:T(8,128)(2,1)}) %all-gather.10.cloned.1.call-update) | async-done | bytes 1572880 | tf_op jit(solution)/shard_map/all_gather | solution.py:88
  177.1 52.5 %while.42 = (s32[]{:T(128)}, f32[3,3,512]{2,1,0:T(4,128)S(1)}, f32[3,3,512]{2,1,0:T(4,128)S(1)}, s32[512]{0:T(512)S(1)}, s32[8]{0:T(128)S(1)}, /*index=5*/s32[40...) while((s32[]{:T(128)}, f32[3,3,512]{2,1,0:T(4,128)S(1)}, ...), condition=%wide.region_8.9_spmd.clone, body=%wide.region_5.0_spmd.clone.sunk | while | flops 321674240 | bytes 21098720 | solution.py:164
  229.6 65.2 %while.43 = (s32[]{:T(128)}, f32[512,3,3,64]{0,3,2,1:T(8,128)}, s32[8]{0:T(128)S(1)}, bf16[4096,192]{0,1:T(8,128)(2,1)}, s32[512]{0:T(512)S(1)}, /*index=5*/s32[...) while((s32[]{:T(128)}, f32[512,3,3,64]{0,3,2,1:T(8,128)}, ...), condition=%wide.region_10.11_spmd.clone, body=%wide.region_9.10_spmd.clone.sunk | while | flops 617153024 | bytes 4690153 | solution.py:191
  232.4 4.3 fusion.134
  239.4 5.6 fusion.134
  247.7 5.6 fusion.134
  256.0 5.6 fusion.134
  264.3 5.6 fusion.134
  272.6 5.6 fusion.134
  280.9 5.6 fusion.134
  289.2 5.6 fusion.134
  297.1 6.7 reshape.421
  303.8 4.9 fusion.71
  308.8 3.6 fusion.56
  312.4 2.8 multiply_reduce_fusion
  319.7 127.2 %while.44 = (s32[]{:T(128)}, f32[512,3,3,64]{0,3,2,1:T(8,128)S(1)}, bf16[8,512,192]{1,2,0:T(8,128)(2,1)}, bf16[8,512,192]{1,2,0:T(8,128)(2,1)}, s32[8]{0:T(128)S...) while((s32[]{:T(128)}, f32[512,3,3,64]{0,3,2,1:T(8,128)S(1)}, ...), condition=%wide.region_15.16_spmd.clone, body=%wide.region_14.15_spmd.clone.sunk | while | flops 1540129280 | bytes 53109092 | solution.py:259
  328.9 3.5 fusion.146
  342.3 2.5 fusion.148
  344.8 3.5 fusion.146
  360.7 3.5 fusion.146
  374.1 2.5 fusion.148
  376.6 3.5 fusion.146
  392.4 3.5 fusion.146
  405.8 2.5 fusion.148
  408.3 3.5 fusion.146
  421.6 2.5 fusion.148
  424.2 3.5 fusion.146
  440.1 3.5 fusion.146
  446.9 2.8 copy.53
  449.7 2.8 copy.54
  452.6 5.0 convolution_bitcast_fusion.1
  457.6 4.5 copy.55
  463.9 3.1 reshape.430
  467.0 4.9 fusion.73
  471.9 5.3 reshape.432
  477.6 35.8 %reduce-scatter.3.cloned.1.call-done = bf16[512,192]{0,1:T(8,128)(2,1)} async-done(((bf16[4096,192]{0,1:T(8,128)(2,1)}), bf16[512,192]{0,1:T(8,128)(2,1)}) %reduce-scatter.3.cloned.1.call-update) | async-done | bytes 196624 | tf_op jit(solution)/shard_map/reduce_scatter | solution.py:260
  514.5 67.1 %reduce-scatter.5.cloned.1.call-done = bf16[512,192]{0,1:T(8,128)(2,1)} async-done(((bf16[4096,192]{0,1:T(8,128)(2,1)}), bf16[512,192]{0,1:T(8,128)(2,1)}) %reduce-scatter.5.cloned.1.call-update) | async-done | bytes 196624 | tf_op jit(solution)/shard_map/reduce_scatter | solution.py:266
  581.6 3.2 fusion.54
  584.8 3.6 reshape.429
  589.2 4.1 fusion.46
  594.3 42.0 %psum.7 = f32[2,576]{1,0:T(2,128)} all-reduce(f32[2,576]{1,0:T(2,128)S(1)} %pad_maximum_fusion.5), channel_id=1, replica_groups=mesh['seq'=8,'dp'=4] {'seq','dp'}, use_global_device_ids=true, to_apply=%region_25.26 | all-reduce | flops 1152 | bytes 9216 | tf_op jit(solution)/shard_map/psum | solution.py:295
  637.7 199.9 %all-reduce.13.cloned.1.call-done = (f32[552960]{0:T(1024)}, f32[331776]{0:T(1024)}, f32[1769472]{0:T(1024)}, f32[884736]{0:T(1024)}) async-done(((f32[552960]{0:T(1024)}, f32[331776]{0:T(1024)}, f32[1769472]{0:T(1024)}, f32[884736]{0:T(1024)}), (f32[552960]{0:T(1024)}, f32[331776]{0:T(1024)}, f32[1769472]{0:T(1024)}, f32[884736]{0:T(1024)})) %all-reduce.13.cloned.1.call-update) | async-done | bytes 14155792
  (430 shorter events, 178.9 us)
Async XLA Ops:
  7.2 63.8 %all-gather.16.cloned.1.call-start = ((), (), s32[]{:S(2)}) async-start(), calls=%async_computation.8 | async-start | bytes 2280960 | tf_op jit(solution)/shard_map/all_gather | solution.py:74
  8.7 129.0 %all-gather.14.cloned.1.call-start = ((), (), s32[]{:S(2)}) async-start(), calls=%async_computation.5 | async-start | bytes 1824768 | tf_op jit(solution)/shard_map/all_gather | solution.py:77
  9.4 167.7 %all-gather.10.cloned.1.call-start = ((), (), s32[]{:S(2)}) async-start(), calls=%async_computation.3 | async-start | bytes 1769472 | tf_op jit(solution)/shard_map/all_gather | solution.py:88
  11.1 68.8 %copy-start.29 = (f32[576]{0:T(1024)}, f32[576]{0:T(1024)S(1)}, u32[]{:S(2)}) copy-start(f32[576]{0:T(1024)S(1)} %get-tuple-element.478) | copy-start | bytes 6916
  13.0 65.7 %copy-start.37 = (f32[512]{0:T(512)}, f32[512]{0:T(512)S(1)}, u32[]{:S(2)}) copy-start(f32[512]{0:T(512)S(1)} %fusion.51) | copy-start | bytes 6148
  13.1 66.8 %copy-start.35 = (f32[512]{0:T(512)}, f32[512]{0:T(512)S(1)}, u32[]{:S(2)}) copy-start(f32[512]{0:T(512)S(1)} %fusion.65) | copy-start | bytes 6148
  13.4 124.0 %copy-start.20 = (f32[512,32]{0,1:T(8,128)}, f32[512,32]{0,1:T(8,128)S(1)}, u32[]{:S(2)}) copy-start(f32[512,32]{0,1:T(8,128)S(1)} %get-tuple-element.574) | copy-start | bytes 196612
  13.4 124.0 %copy-start.22 = (f32[512,32]{0,1:T(8,128)}, f32[512,32]{0,1:T(8,128)S(1)}, u32[]{:S(2)}) copy-start(f32[512,32]{0,1:T(8,128)S(1)} %get-tuple-element.575) | copy-start | bytes 196612
  82.2 3.4 copy-start.34
  83.0 146.6 %all-gather.8.cloned.1.call-start = ((), (), s32[]{:S(2)}) async-start(), calls=%async_computation.2 | async-start | bytes 1769472 | tf_op jit(solution)/shard_map/all_gather | solution.py:89
  84.8 212.2 %all-gather.12.cloned.1.call-start = ((), (), s32[]{:S(2)}) async-start(), calls=%async_computation.4 | async-start | bytes 3649536 | tf_op jit(solution)/shard_map/all_gather | solution.py:76
  85.4 428.0 %reduce-scatter.3.cloned.1.call-start = ((), (), s32[]{:S(2)}) async-start(), calls=%async_computation.6 | async-start | bytes 1769472 | tf_op jit(solution)/shard_map/reduce_scatter | solution.py:260
  134.6 2.8 slice-start
  294.8 1.5 copy-start.6
  303.8 5.0 copy-start.15
  303.8 5.0 copy-start.19
  308.8 3.6 copy-start.3
  312.4 2.8 copy-start.13
  312.4 2.8 copy-start.14
  316.3 2.7 copy-start
  316.3 1.9 copy-start.10
  317.0 2.7 copy-start.17
  324.9 1.5 copy-start.18
  326.4 2.5 copy-start.31
  342.3 2.5 copy-start.31
  358.2 2.5 copy-start.31
  374.0 2.5 copy-start.31
  389.9 2.5 copy-start.31
  405.8 2.5 copy-start.31
  421.6 2.5 copy-start.31
  437.5 2.5 copy-start.31
  449.7 131.9 %reduce-scatter.5.cloned.1.call-start = ((), (), s32[]{:S(2)}) async-start(), calls=%async_computation.7 | async-start | bytes 1769472 | tf_op jit(solution)/shard_map/reduce_scatter | solution.py:266
  452.5 385.0 %all-reduce.13.cloned.1.call-start = ((), (), s32[]{:S(2)}) async-start(), calls=%async_computation.9 | async-start | bytes 28311552
  457.6 4.5 copy-start.1
  457.6 4.5 copy-start.9
  463.9 3.1 copy-start.16
  471.9 5.3 copy-start.21
  471.9 5.3 copy-start.23
  477.5 104.1 %copy-start.30 = (f32[576]{0:T(1024)S(1)}, f32[576]{0:T(1024)}, u32[]{:S(2)}) copy-start(f32[576]{0:T(1024)} %copy-done.29) | copy-start | bytes 6916
  477.5 104.1 %copy-start.36 = (f32[512]{0:T(512)S(1)}, f32[512]{0:T(512)}, u32[]{:S(2)}) copy-start(f32[512]{0:T(512)} %copy-done.35) | copy-start | bytes 6148
  477.6 107.3 %copy-start.24 = (bf16[512,9,64]{0,2,1:T(8,128)(2,1)}, bf16[512,9,64]{0,2,1:T(8,128)(2,1)S(1)}, u32[]{:S(2)}) copy-start(bf16[512,9,64]{0,2,1:T(8,128)(2,1)S(1)} %add_convert_fusion.1) | copy-start | bytes 1769476
  514.4 70.4 %copy-start.26 = (bf16[512,3,64]{0,2,1:T(8,128)(2,1)}, bf16[512,3,64]{0,2,1:T(8,128)(2,1)S(1)}, u32[]{:S(2)}) copy-start(bf16[512,3,64]{0,2,1:T(8,128)(2,1)S(1)} %add_convert_fusion.5) | copy-start | bytes 589828
  589.1 4.1 copy-start.12
  589.1 4.1 copy-start.25
  589.1 4.1 copy-start.27
  589.1 4.1 copy-start.40
  593.3 43.0 %copy-start.38 = (f32[512]{0:T(512)S(1)}, f32[512]{0:T(512)}, u32[]{:S(2)}) copy-start(f32[512]{0:T(512)} %copy-done.37) | copy-start | bytes 6148
  593.3 43.1 %copy-start.2 = (f32[512,576]{0,1:T(8,128)S(1)}, f32[512,576]{0,1:T(8,128)}, u32[]{:S(2)}) copy-start(f32[512,576]{0,1:T(8,128)} %copy-done) | copy-start | bytes 3538948
  (23 other events, 30.8 us)
Sparse Core Ops, SparseCore 0:
  11.4 59.5 all-gather.15
  73.8 55.3 all-gather.13
  131.9 45.1 all-gather.9
  179.6 43.4 all-gather.7
  225.8 58.3 all-gather.11
  449.8 63.5 reduce-scatter.2
  517.2 64.3 reduce-scatter.4
  588.6 248.9 all-reduce.12
